TPU v7x, 32 devices: a whole 2x2x4 slice. The times are simulated.
32 devices in a mesh: ctx: 16 (over z, y, x), kv: 2 (over core).
Axes of the slice: x: 2, y: 2, z: 4, core: 2. Of those that a mesh axis runs over, the one named last changes fastest.
Arguments:
- queries: bfloat16 [4096, 2048], P(('ctx', 'kv')), may hold values from -27 to 27
- key_states: bfloat16 [4096, 256], P(('ctx', 'kv')), may hold values from -12 to 12
- value_states: bfloat16 [4096, 256], P(('ctx', 'kv')), may hold values from -6 to 6
- out_grad: bfloat16 [4096, 2048], P(('ctx', 'kv')), may hold values from -6 to 6
- doc_lengths: int32 [8], replicated, may hold values from 1 to 1024, 4096 in all
Outputs:
- attention: bfloat16 [4096, 2048], P(('ctx', 'kv'))
- query_grad: bfloat16 [4096, 2048], P(('ctx', 'kv'))
- key_grad: bfloat16 [4096, 256], P(('ctx', 'kv'))
- value_grad: bfloat16 [4096, 256], P(('ctx', 'kv'))
Inputs may be any that keep to these rules, and one draw needn't show every extreme that they name: `doc_lengths`: the lengths sum to 4096; the largest is exactly 1024.
All inputs are finite; a program needn't handle non-finite values.
Results may differ from a plain program's by a relative error of at most 0.018.
Values may be sent and summed in bfloat16 or wider, within the bound.
A program may use at most 64 MiB of HBM per device.

v0:
```python
import math

import jax
import jax.numpy as jnp
from jax import lax
from jax.sharding import PartitionSpec as P

HEAD_DIM = 128
DOC_MAX = 1024


def shifted(value, axis, by):
    length = lax.axis_size(axis)
    pairs = [(i, i + by) for i in range(length) if 0 <= i + by < length]
    return lax.ppermute(value, axis, pairs)


def contract_last(left, right):
    return lax.dot_general(
        left, right, (((1,), (1,)), ((), ())), preferred_element_type=jnp.float32
    )


def contract_first(left, right):
    return lax.dot_general(
        left, right, (((0,), (0,)), ((), ())), preferred_element_type=jnp.float32
    )


def doc_index(positions, doc_ends):
    return jnp.sum((doc_ends[None, :] <= positions[:, None]).astype(jnp.int32), axis=1)


def window_mask(first_row, block_rows, reach_back, doc_ends):
    query_pos = first_row + jnp.arange(block_rows, dtype=jnp.int32)
    key_pos = (
        first_row
        - reach_back * block_rows
        + jnp.arange((reach_back + 1) * block_rows, dtype=jnp.int32)
    )
    same_doc = doc_index(query_pos, doc_ends)[:, None] == doc_index(key_pos, doc_ends)[None, :]
    return same_doc & (key_pos[None, :] <= query_pos[:, None]) & (key_pos[None, :] >= 0)


def attend(query_mat, grad_mat, key_mat, value_mat, allowed, groups):
    block_rows = query_mat.shape[0]
    window = key_mat.shape[0]
    head_size = key_mat.shape[1] // groups
    head_count = query_mat.shape[1] // head_size
    per_group = head_count // groups
    stacked = math.gcd(per_group, max(1, 512 // block_rows))
    rounds = head_count // stacked
    factor = 1.0 / math.sqrt(head_size)
    full_mask = jnp.tile(allowed, (stacked, 1))

    def to_rounds(matrix):
        shaped = matrix.reshape(block_rows, rounds, stacked, head_size)
        return jnp.moveaxis(shaped, 0, 2).reshape(rounds, stacked * block_rows, head_size)

    def from_rounds(matrix):
        shaped = matrix.reshape(rounds, stacked, block_rows, head_size)
        return jnp.moveaxis(shaped, 2, 0).reshape(block_rows, head_count * head_size)

    def one_round(totals, inputs):
        key_acc, value_acc = totals
        round_id, query_rows, grad_rows = inputs
        scores = contract_last(query_rows, key_mat) * factor
        highest = jnp.max(jnp.where(full_mask, scores, -jnp.inf), axis=1, keepdims=True)
        expsum = jnp.sum(
            jnp.where(full_mask, jnp.exp(scores - highest), 0.0), axis=1, keepdims=True
        )
        log_total = highest + jnp.log(expsum)
        prob_rows = jnp.where(full_mask, jnp.exp(scores - log_total), 0.0)
        probs_low = prob_rows.astype(jnp.bfloat16)
        output = jnp.dot(probs_low, value_mat, preferred_element_type=jnp.float32).astype(
            jnp.bfloat16
        )
        row_dot = jnp.sum(
            grad_rows.astype(jnp.float32) * output.astype(jnp.float32), axis=1, keepdims=True
        )
        grad_probs = contract_last(grad_rows, value_mat)
        grad_scores = (prob_rows * (grad_probs - row_dot)).astype(jnp.bfloat16)
        query_grad = (
            jnp.dot(grad_scores, key_mat, preferred_element_type=jnp.float32) * factor
        ).astype(jnp.bfloat16)
        key_term = contract_first(grad_scores, query_rows) * factor
        value_term = contract_first(probs_low, grad_rows)
        key_acc = key_acc + key_term
        value_acc = value_acc + value_term
        return ((key_acc, value_acc), (output, query_grad))

    zeros_acc = jnp.zeros((window, groups * head_size), jnp.float32)
    inputs = (jnp.arange(rounds, dtype=jnp.int32), to_rounds(query_mat), to_rounds(grad_mat))
    (key_acc, value_acc), (outputs, query_grads) = lax.scan(
        one_round, (zeros_acc, zeros_acc), inputs
    )
    return (from_rounds(outputs), from_rounds(query_grads), key_acc, value_acc)


def local_attention(
    query_mat, grad_mat, key_mat, value_mat, first_row, reach_back, doc_ends, groups
):
    block_rows = query_mat.shape[0]
    allowed = window_mask(first_row, block_rows, reach_back, doc_ends)
    return attend(query_mat, grad_mat, key_mat, value_mat, allowed, groups)


def body(queries, key_states, value_states, out_grad, doc_lengths):
    doc_ends = jnp.cumsum(doc_lengths)
    query_loc, key_loc, value_loc, grad_loc = (
        lax.all_to_all(queries, "kv", split_axis=1, concat_axis=0, tiled=True),
        lax.all_to_all(key_states, "kv", split_axis=1, concat_axis=0, tiled=True),
        lax.all_to_all(value_states, "kv", split_axis=1, concat_axis=0, tiled=True),
        lax.all_to_all(out_grad, "kv", split_axis=1, concat_axis=0, tiled=True),
    )
    block_rows = query_loc.shape[0]
    reach_back = (DOC_MAX - 1) // block_rows + 1
    first_row = lax.axis_index("ctx") * block_rows
    key_value = jnp.stack([key_loc, value_loc])
    pieces = []
    for offset in range(reach_back, 0, -1):
        pieces.append(shifted(key_value, "ctx", offset))
    pieces.append(key_value)
    window_pair = jnp.concatenate(pieces, axis=1)
    groups = key_loc.shape[1] // HEAD_DIM
    attention, query_grad, key_part, value_part = local_attention(
        query_loc, grad_loc, window_pair[0], window_pair[1], first_row, reach_back, doc_ends, groups
    )
    parts = jnp.stack([key_part, value_part])
    summed = parts[:, reach_back * block_rows :]
    for offset in range(1, reach_back + 1):
        tile_rows = parts[
            :, (reach_back - offset) * block_rows : (reach_back - offset + 1) * block_rows
        ]
        summed = summed + shifted(tile_rows, "ctx", -offset)
    rounded = summed.astype(jnp.bfloat16)
    return (
        lax.all_to_all(attention, "kv", split_axis=0, concat_axis=1, tiled=True),
        lax.all_to_all(query_grad, "kv", split_axis=0, concat_axis=1, tiled=True),
        lax.all_to_all(rounded[0], "kv", split_axis=0, concat_axis=1, tiled=True),
        lax.all_to_all(rounded[1], "kv", split_axis=0, concat_axis=1, tiled=True),
    )


def solution(mesh):
    in_specs = (
        P(("ctx", "kv"), None),
        P(("ctx", "kv"), None),
        P(("ctx", "kv"), None),
        P(("ctx", "kv"), None),
        P(),
    )
    out_specs = (
        P(("ctx", "kv"), None),
        P(("ctx", "kv"), None),
        P(("ctx", "kv"), None),
        P(("ctx", "kv"), None),
    )
    return jax.shard_map(body, mesh=mesh, in_specs=in_specs, out_specs=out_specs, check_vma=False)
```

profile of v0, /device:TPU:0, one launch (start us, length us, event | category | flops | bytes accessed | tf_op | source)
XLA Modules:
  0.0 151.5 jit_solution(6198659562686931299)
XLA Ops:
  2.1 3.3 %all-to-all-start.1 = ((bf16[128,2,128]{2,0,1:T(8,128)(2,1)}), bf16[128,2,128]{2,0,1:T(8,128)(2,1)S(1)}, u32[]{:S(2)}, u32[]{:S(2)}) async-start(bf16[128,2,128]{2,0,1:T(8,128)(2,1)} %copy_bitcast_fusion.4), calls=%async_computation.1 | async-start | bytes 131072 | tf_op jit(solution)/shard_map/all_to_all | solution.py:112
  6.8 3.8 %all_to_all.140 = bf16[128,2,128]{2,0,1:T(8,128)(2,1)S(1)} all-to-all(bf16[128,2,128]{2,0,1:T(8,128)(2,1)S(1)} %copy_bitcast_fusion.3), channel_id=1, replica_groups=mesh['ctx'=16,'kv'=2] {'kv'}, dimensions={1} | all-to-all | bytes 131072 | tf_op jit(solution)/shard_map/all_to_all | solution.py:113
  10.6 4.9 %collective-permute-start = (bf16[2,256,128]{2,1,0:T(8,128)(2,1)S(1)}, bf16[2,256,128]{2,1,0:T(8,128)(2,1)S(1)}, u32[]{:S(2)}, u32[]{:S(2)}) collective-permute-start(bf16[2,256,128]{2,1,0:T(8,128)(2,1)S(1)} %pad_maximum_fusion.1), channel_id=1, source_target_pairs={{0,8},{2,10},{4,12},{6,14},{8,16},{10,18},{12,20},{14,22},{16,24},... | collective-permute-start | bytes 393224 | tf_op jit(solution)/shard_map/ppermute | solution.py:15
  15.6 4.4 %collective-permute-start.1 = (bf16[2,256,128]{2,1,0:T(8,128)(2,1)S(1)}, bf16[2,256,128]{2,1,0:T(8,128)(2,1)S(1)}, u32[]{:S(2)}, u32[]{:S(2)}) collective-permute-start(bf16[2,256,128]{2,1,0:T(8,128)(2,1)S(1)} %pad_maximum_fusion.1), channel_id=1, source_target_pairs={{0,6},{2,8},{4,10},{6,12},{8,14},{10,16},{12,18},{14,20},{16,22},{... | collective-permute-start | bytes 393224 | tf_op jit(solution)/shard_map/ppermute | solution.py:15
  19.9 3.4 %collective-permute-start.2 = (bf16[2,256,128]{2,1,0:T(8,128)(2,1)S(1)}, bf16[2,256,128]{2,1,0:T(8,128)(2,1)S(1)}, u32[]{:S(2)}, u32[]{:S(2)}) collective-permute-start(bf16[2,256,128]{2,1,0:T(8,128)(2,1)S(1)} %pad_maximum_fusion.1), channel_id=1, source_target_pairs={{0,4},{2,6},{4,8},{6,10},{8,12},{10,14},{12,16},{14,18},{16,20},{1... | collective-permute-start | bytes 393224 | tf_op jit(solution)/shard_map/ppermute | solution.py:15
  23.4 2.5 %collective-permute-start.3 = (bf16[2,256,128]{2,1,0:T(8,128)(2,1)S(1)}, bf16[2,256,128]{2,1,0:T(8,128)(2,1)S(1)}, u32[]{:S(2)}, u32[]{:S(2)}) collective-permute-start(bf16[2,256,128]{2,1,0:T(8,128)(2,1)S(1)} %pad_maximum_fusion.1), channel_id=1, source_target_pairs={{0,2},{2,4},{4,6},{6,8},{8,10},{10,12},{12,14},{14,16},{16,18},{18... | collective-permute-start | bytes 393224 | tf_op jit(solution)/shard_map/ppermute | solution.py:15
  27.7 3.5 %all-to-all-start.3 = ((bf16[128,2,1024]{2,0,1:T(8,128)(2,1)}), bf16[128,2,1024]{2,0,1:T(8,128)(2,1)S(1)}, u32[]{:S(2)}, u32[]{:S(2)}) async-start(bf16[128,2,1024]{2,0,1:T(8,128)(2,1)} %bitcast.89), calls=%async_computation.3 | async-start | bytes 1048576 | tf_op jit(solution)/shard_map/all_to_all | solution.py:114
  33.0 3.5 %all-to-all-start = ((bf16[128,2,1024]{2,0,1:T(8,128)(2,1)}), bf16[128,2,1024]{2,0,1:T(8,128)(2,1)S(1)}, u32[]{:S(2)}, u32[]{:S(2)}) async-start(bf16[128,2,1024]{2,0,1:T(8,128)(2,1)} %bitcast.90), calls=%async_computation | async-start | bytes 1048576 | tf_op jit(solution)/shard_map/all_to_all | solution.py:111
  40.4 66.7 %while.17 = (s32[]{:T(128)}, f32[1280,128]{1,0:T(8,128)}, f32[1280,128]{1,0:T(8,128)}, bf16[4,512,128]{1,2,0:T(8,128)(2,1)}, bf16[4,512,128]{2,1,0:T(8,128)(2,1)...) while((s32[]{:T(128)}, f32[1280,128]{1,0:T(8,128)}, ...), condition=%wide.region_7.8_spmd.clone, body=%wide.region_3.7_spmd.clone.sunk | while | flops 1016429568 | bytes 34689208 | solution.py:94
  49.1 2.8 %fusion.66 = f32[1280,128]{1,0:T(8,128)} fusion(bf16[512,1280]{1,0:T(8,128)(2,1)} %fusion.65, f32[1280,128]{1,0:T(8,128)} %get-tuple-element.289, pred[]{:T(512)S(6)} %compare.3, bf16[4,512,128]{2,1,0:T(8,128)(2,1)} %get-tuple-element.305, s32[]{:T(128)} %get-tuple-element.288), kind=kOutput, calls=%fused_computation.12.clone.1 | convolution fusion | flops 168263680 | bytes 2753025 | tf_op jit(solution)/shard_map/while/body/eval_jaxpr/dot_general | solution.py:25
  51.9 2.1 %fusion.67 = bf16[4,512,128]{2,1,0:T(8,128)(2,1)} fusion(bf16[4,512,128]{2,1,0:T(8,128)(2,1)} %get-tuple-element.292, s32[]{:T(128)} %get-tuple-element.288, bf16[512,1280]{1,0:T(8,128)(2,1)S(1)} %copy-done.1, bf16[1280,128]{1,0:T(8,128)(2,1)} %get-tuple-element.306), kind=kOutput, calls=%fused_computation.17.clone.1 | convolution fusion | flops 167903232 | bytes 1769984 | tf_op jit(solution)/shard_map/while/body/eval_jaxpr/dot_general | solution.py:84
  64.8 3.0 %fusion.66 = f32[1280,128]{1,0:T(8,128)} fusion(bf16[512,1280]{1,0:T(8,128)(2,1)} %fusion.65, f32[1280,128]{1,0:T(8,128)} %get-tuple-element.289, pred[]{:T(512)S(6)} %compare.3, bf16[4,512,128]{2,1,0:T(8,128)(2,1)} %get-tuple-element.305, s32[]{:T(128)} %get-tuple-element.288), kind=kOutput, calls=%fused_computation.12.clone.1 | convolution fusion | flops 168263680 | bytes 2753025 | tf_op jit(solution)/shard_map/while/body/eval_jaxpr/dot_general | solution.py:25
  67.8 2.1 %fusion.67 = bf16[4,512,128]{2,1,0:T(8,128)(2,1)} fusion(bf16[4,512,128]{2,1,0:T(8,128)(2,1)} %get-tuple-element.292, s32[]{:T(128)} %get-tuple-element.288, bf16[512,1280]{1,0:T(8,128)(2,1)S(1)} %copy-done.1, bf16[1280,128]{1,0:T(8,128)(2,1)} %get-tuple-element.306), kind=kOutput, calls=%fused_computation.17.clone.1 | convolution fusion | flops 167903232 | bytes 1769984 | tf_op jit(solution)/shard_map/while/body/eval_jaxpr/dot_general | solution.py:84
  70.6 2.5 %convolution_add_fusion.2 = f32[1280,128]{1,0:T(8,128)} fusion(f32[1280,128]{1,0:T(8,128)} %get-tuple-element.290, f32[512,1280]{1,0:T(8,128)S(1)} %bitcast_select_fusion.4, pred[]{:T(512)S(6)} %compare.3, bf16[1,512,128]{2,1,0:T(8,128)(2,1)S(1)} %constant_dynamic-slice_fusion.2), kind=kOutput, calls=%fused_computation.10.clone.1 | convolution fusion | flops 168755200 | bytes 4063233 | tf_op jit(solution)/shard_map/while/body/eval_jaxpr/dot_general | solution.py:25
  81.8 3.0 %fusion.66 = f32[1280,128]{1,0:T(8,128)} fusion(bf16[512,1280]{1,0:T(8,128)(2,1)} %fusion.65, f32[1280,128]{1,0:T(8,128)} %get-tuple-element.289, pred[]{:T(512)S(6)} %compare.3, bf16[4,512,128]{2,1,0:T(8,128)(2,1)} %get-tuple-element.305, s32[]{:T(128)} %get-tuple-element.288), kind=kOutput, calls=%fused_computation.12.clone.1 | convolution fusion | flops 168263680 | bytes 2753025 | tf_op jit(solution)/shard_map/while/body/eval_jaxpr/dot_general | solution.py:25
  87.6 2.5 %convolution_add_fusion.2 = f32[1280,128]{1,0:T(8,128)} fusion(f32[1280,128]{1,0:T(8,128)} %get-tuple-element.290, f32[512,1280]{1,0:T(8,128)S(1)} %bitcast_select_fusion.4, pred[]{:T(512)S(6)} %compare.3, bf16[1,512,128]{2,1,0:T(8,128)(2,1)S(1)} %constant_dynamic-slice_fusion.2), kind=kOutput, calls=%fused_computation.10.clone.1 | convolution fusion | flops 168755200 | bytes 4063233 | tf_op jit(solution)/shard_map/while/body/eval_jaxpr/dot_general | solution.py:25
  98.8 3.0 %fusion.66 = f32[1280,128]{1,0:T(8,128)} fusion(bf16[512,1280]{1,0:T(8,128)(2,1)} %fusion.65, f32[1280,128]{1,0:T(8,128)} %get-tuple-element.289, pred[]{:T(512)S(6)} %compare.3, bf16[4,512,128]{2,1,0:T(8,128)(2,1)} %get-tuple-element.305, s32[]{:T(128)} %get-tuple-element.288), kind=kOutput, calls=%fused_computation.12.clone.1 | convolution fusion | flops 168263680 | bytes 2753025 | tf_op jit(solution)/shard_map/while/body/eval_jaxpr/dot_general | solution.py:25
  101.8 2.1 %fusion.67 = bf16[4,512,128]{2,1,0:T(8,128)(2,1)} fusion(bf16[4,512,128]{2,1,0:T(8,128)(2,1)} %get-tuple-element.292, s32[]{:T(128)} %get-tuple-element.288, bf16[512,1280]{1,0:T(8,128)(2,1)S(1)} %copy-done.1, bf16[1280,128]{1,0:T(8,128)(2,1)} %get-tuple-element.306), kind=kOutput, calls=%fused_computation.17.clone.1 | convolution fusion | flops 167903232 | bytes 1769984 | tf_op jit(solution)/shard_map/while/body/eval_jaxpr/dot_general | solution.py:84
  104.6 2.5 %convolution_add_fusion.2 = f32[1280,128]{1,0:T(8,128)} fusion(f32[1280,128]{1,0:T(8,128)} %get-tuple-element.290, f32[512,1280]{1,0:T(8,128)S(1)} %bitcast_select_fusion.4, pred[]{:T(512)S(6)} %compare.3, bf16[1,512,128]{2,1,0:T(8,128)(2,1)S(1)} %constant_dynamic-slice_fusion.2), kind=kOutput, calls=%fused_computation.10.clone.1 | convolution fusion | flops 168755200 | bytes 4063233 | tf_op jit(solution)/shard_map/while/body/eval_jaxpr/dot_general | solution.py:25
  116.0 4.2 %all_to_all.141 = bf16[2,128,1024]{2,1,0:T(8,128)(2,1)S(1)} all-to-all(bf16[2,128,1024]{2,1,0:T(8,128)(2,1)S(1)} %all_to_all.116), channel_id=1, replica_groups=mesh['ctx'=16,'kv'=2] {'kv'}, dimensions={0} | all-to-all | bytes 1048576 | tf_op jit(solution)/shard_map/all_to_all | solution.py:138
  122.4 4.2 %all_to_all.142 = bf16[2,128,1024]{2,1,0:T(8,128)(2,1)S(1)} all-to-all(bf16[2,128,1024]{2,1,0:T(8,128)(2,1)S(1)} %all_to_all.120), channel_id=1, replica_groups=mesh['ctx'=16,'kv'=2] {'kv'}, dimensions={0} | all-to-all | bytes 1048576 | tf_op jit(solution)/shard_map/all_to_all | solution.py:139
  128.8 12.3 %collective-permute-done.7 = f32[2,256,128]{2,1,0:T(8,128)} collective-permute-done((f32[2,256,128]{2,1,0:T(8,128)S(1)}, f32[2,256,128]{2,1,0:T(8,128)}, u32[]{:S(2)}, u32[]{:S(2)}) %collective-permute-start.7) | collective-permute-done | bytes 262176 | tf_op jit(solution)/shard_map/ppermute | solution.py:15
  142.2 3.8 %all_to_all.143 = bf16[2,128,128]{2,1,0:T(8,128)(2,1)S(1)} all-to-all(bf16[2,128,128]{2,1,0:T(8,128)(2,1)S(1)} %bitcast.147), channel_id=1, replica_groups=mesh['ctx'=16,'kv'=2] {'kv'}, dimensions={0} | all-to-all | bytes 131072 | tf_op jit(solution)/shard_map/all_to_all | solution.py:140
  146.9 3.8 %all_to_all.144 = bf16[2,128,128]{2,1,0:T(8,128)(2,1)S(1)} all-to-all(bf16[2,128,128]{2,1,0:T(8,128)(2,1)S(1)} %bitcast.146), channel_id=1, replica_groups=mesh['ctx'=16,'kv'=2] {'kv'}, dimensions={0} | all-to-all | bytes 131072 | tf_op jit(solution)/shard_map/all_to_all | solution.py:141
  (122 shorter events, 67.2 us)
Async XLA Ops:
  0.6 30.6 %copy-start.7 = (s32[8]{0:T(128)S(1)}, s32[8]{0:T(128)}, u32[]{:S(2)}) copy-start(s32[8]{0:T(128)} %param.11) | copy-start | bytes 100
  1.5 30.6 %copy-start.4 = (bf16[128,2048]{1,0:T(8,128)(2,1)S(1)}, bf16[128,2048]{1,0:T(8,128)(2,1)}, u32[]{:S(2)}) copy-start(bf16[128,2048]{1,0:T(8,128)(2,1)} %param.7) | copy-start | bytes 1572868
  2.1 4.7 %all-to-all-start.1 = ((bf16[128,2,128]{2,0,1:T(8,128)(2,1)}), bf16[128,2,128]{2,0,1:T(8,128)(2,1)S(1)}, u32[]{:S(2)}, u32[]{:S(2)}) async-start(bf16[128,2,128]{2,0,1:T(8,128)(2,1)} %copy_bitcast_fusion.4), calls=%async_computation.1 | async-start | bytes 131072 | tf_op jit(solution)/shard_map/all_to_all | solution.py:112
  10.6 28.8 %collective-permute-start = (bf16[2,256,128]{2,1,0:T(8,128)(2,1)S(1)}, bf16[2,256,128]{2,1,0:T(8,128)(2,1)S(1)}, u32[]{:S(2)}, u32[]{:S(2)}) collective-permute-start(bf16[2,256,128]{2,1,0:T(8,128)(2,1)S(1)} %pad_maximum_fusion.1), channel_id=1, source_target_pairs={{0,8},{2,10},{4,12},{6,14},{8,16},{10,18},{12,20},{14,22},{16,24},... | collective-permute-start | bytes 393224 | tf_op jit(solution)/shard_map/ppermute | solution.py:15
  15.6 23.9 %collective-permute-start.1 = (bf16[2,256,128]{2,1,0:T(8,128)(2,1)S(1)}, bf16[2,256,128]{2,1,0:T(8,128)(2,1)S(1)}, u32[]{:S(2)}, u32[]{:S(2)}) collective-permute-start(bf16[2,256,128]{2,1,0:T(8,128)(2,1)S(1)} %pad_maximum_fusion.1), channel_id=1, source_target_pairs={{0,6},{2,8},{4,10},{6,12},{8,14},{10,16},{12,18},{14,20},{16,22},{... | collective-permute-start | bytes 393224 | tf_op jit(solution)/shard_map/ppermute | solution.py:15
  19.9 19.6 %collective-permute-start.2 = (bf16[2,256,128]{2,1,0:T(8,128)(2,1)S(1)}, bf16[2,256,128]{2,1,0:T(8,128)(2,1)S(1)}, u32[]{:S(2)}, u32[]{:S(2)}) collective-permute-start(bf16[2,256,128]{2,1,0:T(8,128)(2,1)S(1)} %pad_maximum_fusion.1), channel_id=1, source_target_pairs={{0,4},{2,6},{4,8},{6,10},{8,12},{10,14},{12,16},{14,18},{16,20},{1... | collective-permute-start | bytes 393224 | tf_op jit(solution)/shard_map/ppermute | solution.py:15
  23.4 16.2 %collective-permute-start.3 = (bf16[2,256,128]{2,1,0:T(8,128)(2,1)S(1)}, bf16[2,256,128]{2,1,0:T(8,128)(2,1)S(1)}, u32[]{:S(2)}, u32[]{:S(2)}) collective-permute-start(bf16[2,256,128]{2,1,0:T(8,128)(2,1)S(1)} %pad_maximum_fusion.1), channel_id=1, source_target_pairs={{0,2},{2,4},{4,6},{6,8},{8,10},{10,12},{12,14},{14,16},{16,18},{18... | collective-permute-start | bytes 393224 | tf_op jit(solution)/shard_map/ppermute | solution.py:15
  27.7 5.2 %all-to-all-start.3 = ((bf16[128,2,1024]{2,0,1:T(8,128)(2,1)}), bf16[128,2,1024]{2,0,1:T(8,128)(2,1)S(1)}, u32[]{:S(2)}, u32[]{:S(2)}) async-start(bf16[128,2,1024]{2,0,1:T(8,128)(2,1)} %bitcast.89), calls=%async_computation.3 | async-start | bytes 1048576 | tf_op jit(solution)/shard_map/all_to_all | solution.py:114
  33.0 5.2 %all-to-all-start = ((bf16[128,2,1024]{2,0,1:T(8,128)(2,1)}), bf16[128,2,1024]{2,0,1:T(8,128)(2,1)S(1)}, u32[]{:S(2)}, u32[]{:S(2)}) async-start(bf16[128,2,1024]{2,0,1:T(8,128)(2,1)} %bitcast.90), calls=%async_computation | async-start | bytes 1048576 | tf_op jit(solution)/shard_map/all_to_all | solution.py:111
  49.1 2.8 %copy-start.1 = (bf16[512,1280]{1,0:T(8,128)(2,1)S(1)}, bf16[512,1280]{1,0:T(8,128)(2,1)}, u32[]{:S(2)}) copy-start(bf16[512,1280]{1,0:T(8,128)(2,1)} %fusion.65) | copy-start | bytes 3932164 | tf_op jit(solution)/shard_map/while
  49.1 5.0 %copy-start.3 = (bf16[512,128]{0,1:T(8,128)(2,1)S(1)}, bf16[512,128]{0,1:T(8,128)(2,1)}, u32[]{:S(2)}) copy-start(bf16[512,128]{0,1:T(8,128)(2,1)} %get-tuple-element.275) | copy-start | bytes 393220 | tf_op jit(solution)/shard_map/while
  64.8 3.0 %copy-start.1 = (bf16[512,1280]{1,0:T(8,128)(2,1)S(1)}, bf16[512,1280]{1,0:T(8,128)(2,1)}, u32[]{:S(2)}) copy-start(bf16[512,1280]{1,0:T(8,128)(2,1)} %fusion.65) | copy-start | bytes 3932164 | tf_op jit(solution)/shard_map/while
  64.8 5.2 %copy-start.3 = (bf16[512,128]{0,1:T(8,128)(2,1)S(1)}, bf16[512,128]{0,1:T(8,128)(2,1)}, u32[]{:S(2)}) copy-start(bf16[512,128]{0,1:T(8,128)(2,1)} %get-tuple-element.275) | copy-start | bytes 393220 | tf_op jit(solution)/shard_map/while
  81.8 3.0 %copy-start.1 = (bf16[512,1280]{1,0:T(8,128)(2,1)S(1)}, bf16[512,1280]{1,0:T(8,128)(2,1)}, u32[]{:S(2)}) copy-start(bf16[512,1280]{1,0:T(8,128)(2,1)} %fusion.65) | copy-start | bytes 3932164 | tf_op jit(solution)/shard_map/while
  81.8 5.2 %copy-start.3 = (bf16[512,128]{0,1:T(8,128)(2,1)S(1)}, bf16[512,128]{0,1:T(8,128)(2,1)}, u32[]{:S(2)}) copy-start(bf16[512,128]{0,1:T(8,128)(2,1)} %get-tuple-element.275) | copy-start | bytes 393220 | tf_op jit(solution)/shard_map/while
  98.8 3.0 %copy-start.1 = (bf16[512,1280]{1,0:T(8,128)(2,1)S(1)}, bf16[512,1280]{1,0:T(8,128)(2,1)}, u32[]{:S(2)}) copy-start(bf16[512,1280]{1,0:T(8,128)(2,1)} %fusion.65) | copy-start | bytes 3932164 | tf_op jit(solution)/shard_map/while
  98.8 5.2 %copy-start.3 = (bf16[512,128]{0,1:T(8,128)(2,1)S(1)}, bf16[512,128]{0,1:T(8,128)(2,1)}, u32[]{:S(2)}) copy-start(bf16[512,128]{0,1:T(8,128)(2,1)} %get-tuple-element.275) | copy-start | bytes 393220 | tf_op jit(solution)/shard_map/while
  107.1 7.3 %copy-start.5 = (bf16[4,512,128]{1,2,0:T(8,128)(2,1)S(1)}, bf16[4,512,128]{1,2,0:T(8,128)(2,1)}, u32[]{:S(2)}) copy-start(bf16[4,512,128]{1,2,0:T(8,128)(2,1)} %get-tuple-element.59) | copy-start | bytes 1572868
  109.2 18.6 %collective-permute-start.4 = (f32[2,256,128]{2,1,0:T(8,128)}, f32[2,256,128]{2,1,0:T(8,128)S(1)}, u32[]{:S(2)}, u32[]{:S(2)}) collective-permute-start(f32[2,256,128]{2,1,0:T(8,128)} %get-tuple-element.199), channel_id=1, source_target_pairs={{2,0},{4,2},{6,4},{8,6},{10,8},{12,10},{14,12},{16,14},{18,16},{20... | collective-permute-start | bytes 786440 | tf_op jit(solution)/shard_map/ppermute | solution.py:15
  110.5 18.3 %collective-permute-start.5 = (f32[2,256,128]{2,1,0:T(8,128)S(1)}, f32[2,256,128]{2,1,0:T(8,128)S(1)}, u32[]{:S(2)}, u32[]{:S(2)}) collective-permute-start(f32[2,256,128]{2,1,0:T(8,128)S(1)} %get-tuple-element.200), channel_id=1, source_target_pairs={{4,0},{6,2},{8,4},{10,6},{12,8},{14,10},{16,12},{18,14},{20,16},{2... | collective-permute-start | bytes 786440 | tf_op jit(solution)/shard_map/ppermute | solution.py:15
  111.8 17.0 %collective-permute-start.6 = (f32[2,256,128]{2,1,0:T(8,128)S(1)}, f32[2,256,128]{2,1,0:T(8,128)S(1)}, u32[]{:S(2)}, u32[]{:S(2)}) collective-permute-start(f32[2,256,128]{2,1,0:T(8,128)S(1)} %get-tuple-element.202), channel_id=1, source_target_pairs={{6,0},{8,2},{10,4},{12,6},{14,8},{16,10},{18,12},{20,14},{22,16},{... | collective-permute-start | bytes 786440 | tf_op jit(solution)/shard_map/ppermute | solution.py:15
  113.1 28.0 %collective-permute-start.7 = (f32[2,256,128]{2,1,0:T(8,128)S(1)}, f32[2,256,128]{2,1,0:T(8,128)}, u32[]{:S(2)}, u32[]{:S(2)}) collective-permute-start(f32[2,256,128]{2,1,0:T(8,128)S(1)} %get-tuple-element.201), channel_id=1, source_target_pairs={{8,0},{10,2},{12,4},{14,6},{16,8},{18,10},{20,12},{22,14},{24,16},... | collective-permute-start | bytes 786440 | tf_op jit(solution)/shard_map/ppermute | solution.py:15
  114.5 6.9 %copy-start.6 = (bf16[4,512,128]{2,1,0:T(8,128)(2,1)S(1)}, bf16[4,512,128]{2,1,0:T(8,128)(2,1)}, u32[]{:S(2)}) copy-start(bf16[4,512,128]{2,1,0:T(8,128)(2,1)} %get-tuple-element.60) | copy-start | bytes 1572868
  121.4 19.7 %copy-start.2 = (f32[1280,128]{1,0:T(8,128)S(1)}, f32[1280,128]{1,0:T(8,128)}, u32[]{:S(2)}) copy-start(f32[1280,128]{1,0:T(8,128)} %get-tuple-element.61) | copy-start | bytes 1966084
  (1 other events, 0.8 us)
where the time goes:
time: 153 us; the launch traced here: 152 us
  matrix products  51.3 us (34%)
  starting transfers between devices  30.7 us (20%)
  local copies, waits for them, and re-layouts  24.6 us (16%)
  blocking collectives  19.7 us (13%)
  waiting for transfers between devices  14.4 us (9%)
  other arithmetic  9.89 us (6%)
    dot_general x8, matrix products, contract_first(): lax.dot_general(left, right, (((0,), (0,)), ((), ())), preferred_element_...  20.8 us
    ppermute x8, starting transfers between devices, shifted(): return lax.ppermute(value, axis, pairs)  20.4 us
    dot_general x8, matrix products, contract_last(): lax.dot_general(left, right, (((1,), (1,)), ((), ())), preferred_element_...  13.5 us
    ppermute x8, waiting for transfers between devices, shifted(): return lax.ppermute(value, axis, pairs)  13.3 us
    dot_general x4, matrix products, one_round(): jnp.dot(grad_scores, key_mat, preferred_element_type=jnp.float32) * factor  8.54 us
    dot_general x4, matrix products, one_round(): jnp.dot(probs_low, value_mat, preferred_element_type=jnp.float32)  8.49 us
    dynamic_slice x8, local copies, waits for them, and re-layouts, attend(): lax.scan(one_round, (zeros_acc, zeros_acc), inputs)  6.74 us
    unnamed x20, local copies, waits for them, and re-layouts  4.44 us
  transfers between devices with their start and end apart: 11, of which 5 were waited for; matrix products, arithmetic and copies ran while one was open for 7% of the time, Pallas kernels for 0%

commit v1 on v0

v1 whole, which is shorter than its diff:
```python
import functools
import math

import jax
import jax.numpy as jnp
from jax import lax
from jax.experimental import pallas as pl
from jax.experimental.pallas import tpu as pltpu
from jax.sharding import PartitionSpec as P

HEAD_DIM = 128
DOC_MAX = 1024
MESH = pl.DeviceIdType.MESH


def dot_last(left, right):
    return lax.dot_general(
        left, right, (((1,), (1,)), ((), ())), preferred_element_type=jnp.float32
    )


def dot_plain(left, right):
    return jnp.dot(left, right, preferred_element_type=jnp.float32)


def kernel(
    n_ctx, reach, heads,
    q_hbm, g_hbm, k_hbm, v_hbm, doc_ref,
    att_hbm, dq_hbm, dk_ref, dv_ref,
    qraw, graw, qst, gst, kwin, vwin, kwin_t, vwin_t, bias, probs, dscores,
    part_out, part_in, att_buf, dq_buf,
    load_sem, kv_send, kv_recv, qg_send, qg_recv, part_send, part_recv, out_send, out_recv, out_sem,
):
    c = lax.axis_index("ctx")
    m = lax.axis_index("kv")
    other = 1 - m
    T = k_hbm.shape[0]
    D = HEAD_DIM
    shard = 2 * T
    half_cols = heads * D
    span = reach * shard + T
    factor = 1.0 / math.sqrt(D)

    def later(j):
        return c + j < n_ctx

    def earlier(j):
        return c >= j

    barrier = pltpu.get_barrier_semaphore()
    pl.semaphore_signal(barrier, inc=1, device_id=(c, other), device_id_type=MESH)
    for j in range(1, reach + 1):
        @pl.when(later(j))
        def _():
            for e in range(2):
                pl.semaphore_signal(barrier, inc=1, device_id=(c + j, e), device_id_type=MESH)

        @pl.when(earlier(j))
        def _():
            for e in range(2):
                pl.semaphore_signal(barrier, inc=1, device_id=(c - j, e), device_id_type=MESH)

    own_cols = pl.ds(pl.multiple_of(m * half_cols, D), half_cols)
    own_key_cols = pl.ds(pl.multiple_of(m * D, D), D)
    own_rows = pl.ds(pl.multiple_of(reach * shard + m * T, T), T)
    loads = [
        pltpu.make_async_copy(k_hbm.at[:, own_key_cols], kwin.at[own_rows], load_sem.at[0]),
        pltpu.make_async_copy(v_hbm.at[:, own_key_cols], vwin.at[own_rows], load_sem.at[1]),
        pltpu.make_async_copy(q_hbm.at[:, own_cols], qraw.at[m], load_sem.at[2]),
        pltpu.make_async_copy(g_hbm.at[:, own_cols], graw.at[m], load_sem.at[3]),
    ]
    for copy in loads:
        copy.start()

    peers = jnp.int32(1)
    for j in range(1, reach + 1):
        peers = peers + jnp.where(later(j), 2, 0) + jnp.where(earlier(j), 2, 0)
    pl.semaphore_wait(barrier, peers)

    def kv_copy(j, dest, sender):
        cols = pl.ds(pl.multiple_of(dest * D, D), D)
        rows = pl.ds(pl.multiple_of((reach - j) * shard + sender * T, T), T)
        copies = []
        for which, (src, dst) in enumerate(((k_hbm, kwin), (v_hbm, vwin))):
            copies.append(
                pltpu.make_async_remote_copy(
                    src_ref=src.at[:, cols],
                    dst_ref=dst.at[rows],
                    send_sem=kv_send.at[(j * 2 + dest) * 2 + which],
                    recv_sem=kv_recv.at[(j * 2 + sender) * 2 + which],
                    device_id=(c + j, dest),
                    device_id_type=MESH,
                )
            )
        return copies

    for j in range(reach, 0, -1):
        @pl.when(later(j))
        def _():
            for dest in range(2):
                for copy in kv_copy(j, dest, m):
                    copy.start()
    for copy in kv_copy(0, other, m):
        copy.start()

    def qg_copies(sender, dest):
        cols = pl.ds(pl.multiple_of(dest * half_cols, D), half_cols)
        copies = []
        for which, (src, dst) in enumerate(((q_hbm, qraw), (g_hbm, graw))):
            copies.append(
                pltpu.make_async_remote_copy(
                    src_ref=src.at[:, cols],
                    dst_ref=dst.at[sender],
                    send_sem=qg_send.at[which],
                    recv_sem=qg_recv.at[which],
                    device_id=(c, dest),
                    device_id_type=MESH,
                )
            )
        return copies

    for copy in qg_copies(m, other):
        copy.start()

    for j in range(1, reach + 1):
        @pl.when(jnp.logical_not(earlier(j)))
        def _():
            rows = pl.ds((reach - j) * shard, shard)
            kwin[rows, :] = jnp.zeros((shard, D), kwin.dtype)
            vwin[rows, :] = jnp.zeros((shard, D), vwin.dtype)

        @pl.when(jnp.logical_not(later(j)))
        def _():
            part_in[j] = jnp.zeros(part_in.shape[1:], part_in.dtype)

    for t in range(2):
        row_pos = c * shard + t * T + lax.broadcasted_iota(jnp.int32, (1, T), 1)
        first = jnp.zeros((1, T), jnp.int32)
        end = jnp.int32(0)
        for d in range(doc_ref.shape[0]):
            end = end + doc_ref[d]
            first = jnp.where(end <= row_pos, end, first)
        key_pos = (c - reach) * shard + t * T + lax.broadcasted_iota(jnp.int32, (span, T), 0)
        allowed = (key_pos >= first) & (key_pos <= row_pos)
        bias[t] = jnp.where(allowed, 0.0, -1e30)

    for copy in loads:
        copy.wait()
    for copy in qg_copies(other, m):
        copy.wait_recv()
    for t in range(2):
        for h in range(heads):
            qst[t, h * T : (h + 1) * T, :] = qraw[t, :, h * D : (h + 1) * D]
            gst[t, h * T : (h + 1) * T, :] = graw[t, :, h * D : (h + 1) * D]
    for copy in kv_copy(0, m, other):
        copy.wait_recv()
    for j in range(1, reach + 1):
        @pl.when(earlier(j))
        def _():
            for sender in range(2):
                for copy in kv_copy(j, m, sender):
                    copy.wait_recv()

    kwin_t[...] = kwin[...].T
    vwin_t[...] = vwin[...].T

    pair = 2 * T
    scale2 = factor * math.log2(math.e)

    for t in range(2):
        keys = slice(t * T, t * T + span)

        def one_pair(i, carry):
            cols = pl.ds(pl.multiple_of(i * pair, pair), pair)
            scores = dot_last(kwin[keys, :], qst[t, cols, :])
            mask_term = bias[t]
            z = scores * scale2 + jnp.concatenate([mask_term, mask_term], axis=1)
            highest = jnp.max(z, axis=0, keepdims=True)
            e = jnp.exp2(z - highest)
            total = jnp.sum(e, axis=0, keepdims=True)
            p = e * (1.0 / total)
            gp = dot_last(vwin[keys, :], gst[t, cols, :])
            row_dot = jnp.sum(p * gp, axis=0, keepdims=True)
            probs[t, :, cols] = p.astype(jnp.bfloat16)
            dscores[t, :, cols] = (p * (gp - row_dot)).astype(jnp.bfloat16)
            return carry

        lax.fori_loop(0, heads // 2, one_pair, 0)

    for which, (lhs, rhs, scale) in enumerate(((dscores, qst, factor), (probs, gst, 1.0))):
        low = dot_plain(lhs[0], rhs[0]) * scale
        high = dot_plain(lhs[1], rhs[1]) * scale
        for block in range(2 * (reach + 1)):
            value = None
            if block < 2 * reach + 1:
                value = low[block * T : (block + 1) * T]
            if block >= 1:
                part = high[(block - 1) * T : block * T]
                value = part if value is None else value + part
            part_out[reach - block // 2, block % 2, which] = value.astype(part_out.dtype)

    def part_copy(j, dest, sender):
        return pltpu.make_async_remote_copy(
            src_ref=part_out.at[j, dest],
            dst_ref=part_in.at[j, sender],
            send_sem=part_send.at[j * 2 + dest],
            recv_sem=part_recv.at[j * 2 + sender],
            device_id=(c - j, dest),
            device_id_type=MESH,
        )

    for j in range(reach, 0, -1):
        @pl.when(earlier(j))
        def _():
            for dest in range(2):
                part_copy(j, dest, m).start()
    part_copy(0, other, m).start()

    def remote_out(sender, dest):
        cols = pl.ds(pl.multiple_of(sender * half_cols, D), half_cols)
        return [
            pltpu.make_async_remote_copy(
                src_ref=src.at[dest],
                dst_ref=dst.at[:, cols],
                send_sem=out_send.at[which],
                recv_sem=out_recv.at[which],
                device_id=(c, dest),
                device_id_type=MESH,
            )
            for which, (src, dst) in enumerate(((att_buf, att_hbm), (dq_buf, dq_hbm)))
        ]

    def outputs(t):
        keys = pl.ds(pl.multiple_of(t * T, T), span)

        def one_pair(i, carry):
            cols = pl.ds(pl.multiple_of(i * pair, pair), pair)
            o = dot_plain(vwin_t[:, keys], probs[t, :, cols]).T
            dq = (dot_plain(kwin_t[:, keys], dscores[t, :, cols]) * factor).T
            for a in range(2):
                at = pl.ds(pl.multiple_of(i * 2 * D + a * D, D), D)
                att_buf[t, :, at] = o[a * T : (a + 1) * T].astype(att_buf.dtype)
                dq_buf[t, :, at] = dq[a * T : (a + 1) * T].astype(dq_buf.dtype)
            return carry

        lax.fori_loop(0, heads // 2, one_pair, 0)

    outputs(other)
    for copy in remote_out(m, other):
        copy.start()
    outputs(m)
    stores = [
        pltpu.make_async_copy(att_buf.at[m], att_hbm.at[:, own_cols], out_sem.at[0]),
        pltpu.make_async_copy(dq_buf.at[m], dq_hbm.at[:, own_cols], out_sem.at[1]),
    ]
    for copy in stores:
        copy.start()

    part_in[0, m] = part_out[0, m]
    part_copy(0, m, other).wait_recv()
    for j in range(1, reach + 1):
        @pl.when(later(j))
        def _():
            for sender in range(2):
                part_copy(j, m, sender).wait_recv()
    for which, ref in enumerate((dk_ref, dv_ref)):
        for e in range(2):
            total = part_in[0, e, which].astype(jnp.float32)
            for j in range(1, reach + 1):
                total = total + part_in[j, e, which].astype(jnp.float32)
            ref[:, e * D : (e + 1) * D] = total.astype(ref.dtype)

    for copy in stores:
        copy.wait()
    for copy in remote_out(other, m):
        copy.wait_recv()
    for copy in remote_out(m, other):
        copy.wait_send()
    for copy in qg_copies(m, other):
        copy.wait_send()
    for copy in kv_copy(0, other, m):
        copy.wait_send()
    part_copy(0, other, m).wait_send()
    for j in range(1, reach + 1):
        @pl.when(later(j))
        def _():
            for dest in range(2):
                for copy in kv_copy(j, dest, m):
                    copy.wait_send()

        @pl.when(earlier(j))
        def _():
            for dest in range(2):
                part_copy(j, dest, m).wait_send()


def solution(mesh):
    n_ctx = mesh.shape["ctx"]

    def body(queries, key_states, value_states, out_grad, doc_lengths):
        T, q_cols = queries.shape
        D = HEAD_DIM
        heads = q_cols // D // 2
        shard = 2 * T
        reach = (DOC_MAX - 1) // shard + 1
        window = (reach + 1) * shard
        span = reach * shard + T
        bf16, f32 = jnp.bfloat16, jnp.float32
        hbm = pl.BlockSpec(memory_space=pl.ANY)
        vmem = pl.BlockSpec(memory_space=pltpu.VMEM)
        dma = pltpu.SemaphoreType.DMA
        return pl.pallas_call(
            functools.partial(kernel, n_ctx, reach, heads),
            out_shape=(
                jax.ShapeDtypeStruct(queries.shape, bf16),
                jax.ShapeDtypeStruct(queries.shape, bf16),
                jax.ShapeDtypeStruct(key_states.shape, bf16),
                jax.ShapeDtypeStruct(key_states.shape, bf16),
            ),
            in_specs=[hbm] * 4 + [pl.BlockSpec(memory_space=pltpu.SMEM)],
            out_specs=(hbm, hbm, vmem, vmem),
            scratch_shapes=[
                pltpu.VMEM((2, T, heads * D), bf16),
                pltpu.VMEM((2, T, heads * D), bf16),
                pltpu.VMEM((2, heads * T, D), bf16),
                pltpu.VMEM((2, heads * T, D), bf16),
                pltpu.VMEM((window, D), bf16),
                pltpu.VMEM((window, D), bf16),
                pltpu.VMEM((D, window), bf16),
                pltpu.VMEM((D, window), bf16),
                pltpu.VMEM((2, span, T), f32),
                pltpu.VMEM((2, span, heads * T), bf16),
                pltpu.VMEM((2, span, heads * T), bf16),
                pltpu.VMEM((reach + 1, 2, 2, T, D), bf16),
                pltpu.VMEM((reach + 1, 2, 2, T, D), bf16),
                pltpu.VMEM((2, T, heads * D), bf16),
                pltpu.VMEM((2, T, heads * D), bf16),
                dma((4,)),
                dma(((reach + 1) * 4,)),
                dma(((reach + 1) * 4,)),
                dma((2,)),
                dma((2,)),
                dma(((reach + 1) * 2,)),
                dma(((reach + 1) * 2,)),
                dma((2,)),
                dma((2,)),
                dma((2,)),
            ],
            compiler_params=pltpu.CompilerParams(
                collective_id=0, has_side_effects=True, vmem_limit_bytes=48 * 1024 * 1024
            ),
        )(queries, out_grad, key_states, value_states, doc_lengths)

    return jax.shard_map(
        body,
        mesh=mesh,
        in_specs=(P(("ctx", "kv"), None),) * 4 + (P(),),
        out_specs=(P(("ctx", "kv"), None),) * 4,
        check_vma=False,
    )
```

time: 153 us -> 52 us (0.34)
  the two profiles are of different devices: /device:TPU:0 before, /device:TPU:7 now
where the time goes in v1:
time: 52 us; the launch traced here: 51.7 us
  Pallas kernels  43.8 us (84%)
  local copies, waits for them, and re-layouts  7.25 us (14%)
  between operations  0.65 us (1%)
    pallas_call x1, Pallas kernels, body(): pl.pallas_call(functools.partial(kernel, n_ctx, reach, heads), out_shape=...  43.8 us
    unnamed x14, local copies, waits for them, and re-layouts  7.25 us

profile of v1, /device:TPU:7, one launch (start us, length us, event | category | flops | bytes accessed | tf_op | source)
XLA Modules:
  0.0 51.7 jit_solution(6544047384798804885)
XLA Ops:
  0.6 0.0 copy-start
  0.6 1.0 %copy-done = bf16[128,2048]{1,0:T(8,128)(2,1)S(1)} copy-done((bf16[128,2048]{1,0:T(8,128)(2,1)S(1)}, bf16[128,2048]{1,0:T(8,128)(2,1)}, u32[]{:S(2)}) %copy-start) | copy-done | bytes 524312
  1.7 0.0 copy-start.1
  1.7 1.0 %copy-done.1 = bf16[128,2048]{1,0:T(8,128)(2,1)S(1)} copy-done((bf16[128,2048]{1,0:T(8,128)(2,1)S(1)}, bf16[128,2048]{1,0:T(8,128)(2,1)}, u32[]{:S(2)}) %copy-start.1) | copy-done | bytes 524312
  2.7 0.0 copy-start.2
  2.7 0.8 %copy-done.2 = bf16[128,256]{1,0:T(8,128)(2,1)S(1)} copy-done((bf16[128,256]{1,0:T(8,128)(2,1)S(1)}, bf16[128,256]{1,0:T(8,128)(2,1)}, u32[]{:S(2)}) %copy-start.2) | copy-done | bytes 65560
  3.6 0.0 copy-start.3
  3.6 0.8 %copy-done.3 = bf16[128,256]{1,0:T(8,128)(2,1)S(1)} copy-done((bf16[128,256]{1,0:T(8,128)(2,1)S(1)}, bf16[128,256]{1,0:T(8,128)(2,1)}, u32[]{:S(2)}) %copy-start.3) | copy-done | bytes 65560
  4.4 0.0 copy-start.4
  4.4 0.7 %copy-done.4 = s32[8]{0:T(128)S(1)} copy-done((s32[8]{0:T(128)S(1)}, s32[8]{0:T(128)}, u32[]{:S(2)}) %copy-start.4) | copy-done | bytes 56
  5.1 43.8 %shard_map.84 = (bf16[128,2048]{1,0:T(8,128)(2,1)S(1)}, bf16[128,2048]{1,0:T(8,128)(2,1)S(1)}, bf16[128,256]{1,0:T(8,128)(2,1)S(1)}, bf16[128,256]{1,0:T(8,128)(2,1)S(1)}) custom-call(bf16[128,2048]{1,0:T(8,128)(2,1)S(1)} %copy-done, bf16[128,2048]{1,0:T(8,128)(2,1)S(1)} %copy-done.1, bf16[128,256]{1,0:T(8,128)(2,1)S(1)} %copy-done.2, ...), custom_call_target="tpu_custom_call" | custom-call | tf_op jit(solution)/shard_map/pallas_call | solution.py:312
  48.9 0.8 %copy.13 = bf16[128,2048]{1,0:T(8,128)(2,1)} copy(bf16[128,2048]{1,0:T(8,128)(2,1)S(1)} %get-tuple-element.8) | data formatting | bytes 1048576
  49.7 0.8 %copy.14 = bf16[128,2048]{1,0:T(8,128)(2,1)} copy(bf16[128,2048]{1,0:T(8,128)(2,1)S(1)} %get-tuple-element.9) | data formatting | bytes 1048576
  50.5 0.6 %copy.15 = bf16[128,256]{1,0:T(8,128)(2,1)} copy(bf16[128,256]{1,0:T(8,128)(2,1)S(1)} %get-tuple-element.10) | data formatting | bytes 131072
  51.1 0.6 %copy.16 = bf16[128,256]{1,0:T(8,128)(2,1)} copy(bf16[128,256]{1,0:T(8,128)(2,1)S(1)} %get-tuple-element.11) | data formatting | bytes 131072
Async XLA Ops:
  0.6 1.0 %copy-start = (bf16[128,2048]{1,0:T(8,128)(2,1)S(1)}, bf16[128,2048]{1,0:T(8,128)(2,1)}, u32[]{:S(2)}) copy-start(bf16[128,2048]{1,0:T(8,128)(2,1)} %q_hbm.1) | copy-start | bytes 1572868
  1.7 1.0 %copy-start.1 = (bf16[128,2048]{1,0:T(8,128)(2,1)S(1)}, bf16[128,2048]{1,0:T(8,128)(2,1)}, u32[]{:S(2)}) copy-start(bf16[128,2048]{1,0:T(8,128)(2,1)} %g_hbm.1) | copy-start | bytes 1572868
  2.7 0.8 %copy-start.2 = (bf16[128,256]{1,0:T(8,128)(2,1)S(1)}, bf16[128,256]{1,0:T(8,128)(2,1)}, u32[]{:S(2)}) copy-start(bf16[128,256]{1,0:T(8,128)(2,1)} %k_hbm.1) | copy-start | bytes 196612
  3.6 0.8 %copy-start.3 = (bf16[128,256]{1,0:T(8,128)(2,1)S(1)}, bf16[128,256]{1,0:T(8,128)(2,1)}, u32[]{:S(2)}) copy-start(bf16[128,256]{1,0:T(8,128)(2,1)} %v_hbm.1) | copy-start | bytes 196612
  4.4 0.7 %copy-start.4 = (s32[8]{0:T(128)S(1)}, s32[8]{0:T(128)}, u32[]{:S(2)}) copy-start(s32[8]{0:T(128)} %doc_ref.1) | copy-start | bytes 100

commit v2 on v1

--- a/solution.py
+++ b/solution.py
@@ -10,6 +10,7 @@
 
 HEAD_DIM = 128
 DOC_MAX = 1024
+STEP = 512
 MESH = pl.DeviceIdType.MESH
 
 
@@ -27,9 +28,11 @@
     n_ctx, reach, heads,
     q_hbm, g_hbm, k_hbm, v_hbm, doc_ref,
     att_hbm, dq_hbm, dk_ref, dv_ref,
-    qraw, graw, qst, gst, kwin, vwin, kwin_t, vwin_t, bias, probs, dscores,
-    part_out, part_in, att_buf, dq_buf,
-    load_sem, kv_send, kv_recv, qg_send, qg_recv, part_send, part_recv, out_send, out_recv, out_sem,
+    qraw, graw, qst, gst, kwin, vwin, kwin_t, vwin_t, bias, exps, gprobs, probs, dscores,
+    block_max, block_sum, block_dot, weight, row_dot,
+    part_out, part_in, agg_in, agg_out, att_buf, dq_buf,
+    load_sem, kv_send, kv_recv, qg_send, qg_recv, relay_send, part_send, part_recv,
+    agg_send, agg_recv, out_send, out_recv, out_sem,
 ):
     c = lax.axis_index("ctx")
     m = lax.axis_index("kv")
@@ -41,24 +44,32 @@
     span = reach * shard + T
     factor = 1.0 / math.sqrt(D)
 
-    def later(j):
-        return c + j < n_ctx
-
-    def earlier(j):
+    place = c % reach
+    has_next = c + reach < n_ctx
+    has_prev = c >= reach
+
+    def sends_to(j):
+        return has_next if j == reach else place + j < reach
+
+    def exists(j):
         return c >= j
 
     barrier = pltpu.get_barrier_semaphore()
     pl.semaphore_signal(barrier, inc=1, device_id=(c, other), device_id_type=MESH)
-    for j in range(1, reach + 1):
-        @pl.when(later(j))
-        def _():
-            for e in range(2):
-                pl.semaphore_signal(barrier, inc=1, device_id=(c + j, e), device_id_type=MESH)
-
-        @pl.when(earlier(j))
-        def _():
-            for e in range(2):
-                pl.semaphore_signal(barrier, inc=1, device_id=(c - j, e), device_id_type=MESH)
+    for j in range(1, reach):
+        for e in range(2):
+            near = c - place + (place + j) % reach
+            pl.semaphore_signal(barrier, inc=1, device_id=(near, e), device_id_type=MESH)
+
+    @pl.when(has_next)
+    def _():
+        for e in range(2):
+            pl.semaphore_signal(barrier, inc=1, device_id=(c + reach, e), device_id_type=MESH)
+
+    @pl.when(has_prev)
+    def _():
+        for e in range(2):
+            pl.semaphore_signal(barrier, inc=1, device_id=(c - reach, e), device_id_type=MESH)
 
     own_cols = pl.ds(pl.multiple_of(m * half_cols, D), half_cols)
     own_key_cols = pl.ds(pl.multiple_of(m * D, D), D)
@@ -72,9 +83,7 @@
     for copy in loads:
         copy.start()
 
-    peers = jnp.int32(1)
-    for j in range(1, reach + 1):
-        peers = peers + jnp.where(later(j), 2, 0) + jnp.where(earlier(j), 2, 0)
+    peers = 1 + 2 * (reach - 1) + jnp.where(has_next, 2, 0) + jnp.where(has_prev, 2, 0)
     pl.semaphore_wait(barrier, peers)
 
     def kv_copy(j, dest, sender):
@@ -94,12 +103,12 @@
             )
         return copies
 
-    for j in range(reach, 0, -1):
-        @pl.when(later(j))
-        def _():
-            for dest in range(2):
-                for copy in kv_copy(j, dest, m):
-                    copy.start()
+    @pl.when(has_next)
+    def _():
+        for dest in range(2):
+            for copy in kv_copy(reach, dest, m):
+                copy.start()
+
     for copy in kv_copy(0, other, m):
         copy.start()
 
@@ -121,17 +130,39 @@
 
     for copy in qg_copies(m, other):
         copy.start()
+    for j in range(1, reach):
+        @pl.when(sends_to(j))
+        def _():
+            for dest in range(2):
+                for copy in kv_copy(j, dest, m):
+                    copy.start()
+
+    def relay_copy(back, sender, which):
+        win = (kwin, vwin)[which]
+        return pltpu.make_async_remote_copy(
+            src_ref=win.at[pl.ds(sender * T, T)],
+            dst_ref=win.at[pl.ds(back * shard + sender * T, T)],
+            send_sem=relay_send.at[(back * 2 + sender) * 2 + which],
+            recv_sem=kv_recv.at[((reach - back) * 2 + sender) * 2 + which],
+            device_id=(c - back, m),
+            device_id_type=MESH,
+        )
 
     for j in range(1, reach + 1):
-        @pl.when(jnp.logical_not(earlier(j)))
+        @pl.when(jnp.logical_not(exists(j)))
         def _():
             rows = pl.ds((reach - j) * shard, shard)
             kwin[rows, :] = jnp.zeros((shard, D), kwin.dtype)
             vwin[rows, :] = jnp.zeros((shard, D), vwin.dtype)
 
-        @pl.when(jnp.logical_not(later(j)))
+        @pl.when(jnp.logical_not(sends_to(j)))
         def _():
             part_in[j] = jnp.zeros(part_in.shape[1:], part_in.dtype)
+
+    for back in range(1, reach):
+        @pl.when(place < back)
+        def _():
+            agg_in[back] = jnp.zeros(agg_in.shape[1:], agg_in.dtype)
 
     for t in range(2):
         row_pos = c * shard + t * T + lax.broadcasted_iota(jnp.int32, (1, T), 1)
@@ -152,52 +183,76 @@
         for h in range(heads):
             qst[t, h * T : (h + 1) * T, :] = qraw[t, :, h * D : (h + 1) * D]
             gst[t, h * T : (h + 1) * T, :] = graw[t, :, h * D : (h + 1) * D]
+    step_cols = min(STEP, heads * T)
+    scale2 = factor * math.log2(math.e)
+
+    def rows_of(j, t):
+        low = max((reach - j) * shard, t * T)
+        high = min((reach - j + 1) * shard, t * T + span)
+        return low, high
+
+    def each_step(run):
+        def one(i, carry):
+            run(pl.ds(pl.multiple_of(i * step_cols, step_cols), step_cols))
+            return carry
+
+        lax.fori_loop(0, heads * T // step_cols, one, 0)
+
+    def score_block(j):
+        for t in range(2):
+            low, high = rows_of(j, t)
+
+            def run(cols):
+                local = slice(low - t * T, high - t * T)
+                scores = dot_last(kwin[low:high, :], qst[t, cols, :])
+                mask_term = jnp.concatenate([bias[t, local, :]] * (step_cols // T), axis=1)
+                z = scores * scale2 + mask_term
+                highest = jnp.max(z, axis=0, keepdims=True)
+                e = jnp.exp2(z - highest)
+                gp = dot_last(vwin[low:high, :], gst[t, cols, :])
+                exps[t, local, cols] = e
+                gprobs[t, local, cols] = gp
+                block_max[j, t, :, cols] = highest
+                block_sum[j, t, :, cols] = jnp.sum(e, axis=0, keepdims=True)
+                block_dot[j, t, :, cols] = jnp.sum(e * gp, axis=0, keepdims=True)
+
+            each_step(run)
+
     for copy in kv_copy(0, m, other):
         copy.wait_recv()
-    for j in range(1, reach + 1):
-        @pl.when(earlier(j))
+    score_block(0)
+
+    @pl.when(has_prev)
+    def _():
+        for sender in range(2):
+            for which, copy in enumerate(kv_copy(reach, m, sender)):
+                copy.wait_recv()
+                for back in range(1, reach):
+                    @pl.when(place >= back)
+                    def _():
+                        relay_copy(back, sender, which).start()
+
+    score_block(reach)
+    for j in range(1, reach):
+        @pl.when(exists(j))
         def _():
             for sender in range(2):
                 for copy in kv_copy(j, m, sender):
                     copy.wait_recv()
 
-    kwin_t[...] = kwin[...].T
-    vwin_t[...] = vwin[...].T
-
-    pair = 2 * T
-    scale2 = factor * math.log2(math.e)
+        score_block(j)
 
     for t in range(2):
-        keys = slice(t * T, t * T + span)
-
-        def one_pair(i, carry):
-            cols = pl.ds(pl.multiple_of(i * pair, pair), pair)
-            scores = dot_last(kwin[keys, :], qst[t, cols, :])
-            mask_term = bias[t]
-            z = scores * scale2 + jnp.concatenate([mask_term, mask_term], axis=1)
-            highest = jnp.max(z, axis=0, keepdims=True)
-            e = jnp.exp2(z - highest)
-            total = jnp.sum(e, axis=0, keepdims=True)
-            p = e * (1.0 / total)
-            gp = dot_last(vwin[keys, :], gst[t, cols, :])
-            row_dot = jnp.sum(p * gp, axis=0, keepdims=True)
-            probs[t, :, cols] = p.astype(jnp.bfloat16)
-            dscores[t, :, cols] = (p * (gp - row_dot)).astype(jnp.bfloat16)
-            return carry
-
-        lax.fori_loop(0, heads // 2, one_pair, 0)
-
-    for which, (lhs, rhs, scale) in enumerate(((dscores, qst, factor), (probs, gst, 1.0))):
-        low = dot_plain(lhs[0], rhs[0]) * scale
-        high = dot_plain(lhs[1], rhs[1]) * scale
-        for block in range(2 * (reach + 1)):
-            value = None
-            if block < 2 * reach + 1:
-                value = low[block * T : (block + 1) * T]
-            if block >= 1:
-                part = high[(block - 1) * T : block * T]
-                value = part if value is None else value + part
-            part_out[reach - block // 2, block % 2, which] = value.astype(part_out.dtype)
+        highest = block_max[0, t]
+        for j in range(1, reach + 1):
+            highest = jnp.maximum(highest, block_max[j, t])
+        shrink = [jnp.exp2(block_max[j, t] - highest) for j in range(reach + 1)]
+        total = sum(block_sum[j, t] * shrink[j] for j in range(reach + 1))
+        inverse = 1.0 / total
+        shrink = [value * inverse for value in shrink]
+        row_dot[t] = sum(block_dot[j, t] * shrink[j] for j in range(reach + 1))
+        for j in range(reach + 1):
+            weight[j, t] = shrink[j]
 
     def part_copy(j, dest, sender):
         return pltpu.make_async_remote_copy(
@@ -209,12 +264,67 @@
             device_id_type=MESH,
         )
 
-    for j in range(reach, 0, -1):
-        @pl.when(earlier(j))
-        def _():
-            for dest in range(2):
-                part_copy(j, dest, m).start()
-    part_copy(0, other, m).start()
+    def agg_copy(back):
+        return pltpu.make_async_remote_copy(
+            src_ref=part_out.at[reach - back],
+            dst_ref=agg_in.at[back],
+            send_sem=agg_send.at[back],
+            recv_sem=agg_recv.at[back],
+            device_id=(c + back, m),
+            device_id_type=MESH,
+        )
+
+    def agg_out_copy(dest, sender):
+        return pltpu.make_async_remote_copy(
+            src_ref=agg_out.at[dest],
+            dst_ref=part_in.at[reach, sender],
+            send_sem=part_send.at[reach * 2 + dest],
+            recv_sem=part_recv.at[reach * 2 + sender],
+            device_id=(c - reach, dest),
+            device_id_type=MESH,
+        )
+
+    for j in range(reach, -1, -1):
+        for t in range(2):
+            low, high = rows_of(j, t)
+
+            def run(cols):
+                local = slice(low - t * T, high - t * T)
+                p = exps[t, local, cols] * weight[j, t, :, cols]
+                probs[t, local, cols] = p.astype(jnp.bfloat16)
+                ds = p * (gprobs[t, local, cols] - row_dot[t, :, cols])
+                dscores[t, local, cols] = ds.astype(jnp.bfloat16)
+
+            each_step(run)
+        for which, (lhs, rhs, scale) in enumerate(((dscores, qst, factor), (probs, gst, 1.0))):
+            value = []
+            for t in range(2):
+                low, high = rows_of(j, t)
+                value.append(dot_plain(lhs[t, low - t * T : high - t * T, :], rhs[t]) * scale)
+            low, high = value
+            if j == 0:
+                halves = (low + high[:T], high[T:])
+            elif j == reach:
+                halves = (low[:T], low[T:] + high)
+            else:
+                halves = (low[:T] + high[:T], low[T:] + high[T:])
+            for half in range(2):
+                part_out[j, half, which] = halves[half].astype(part_out.dtype)
+        if j == 0:
+            part_copy(0, other, m).start()
+        elif j < reach:
+            @pl.when(place >= j)
+            def _():
+                for dest in range(2):
+                    part_copy(j, dest, m).start()
+
+            @pl.when((place < j) & has_prev)
+            def _():
+                agg_copy(reach - j).start()
+
+    kwin_t[...] = kwin[...].T
+    vwin_t[...] = vwin[...].T
+    pair = 2 * T
 
     def remote_out(sender, dest):
         cols = pl.ds(pl.multiple_of(sender * half_cols, D), half_cols)
@@ -248,6 +358,22 @@
     outputs(other)
     for copy in remote_out(m, other):
         copy.start()
+
+    @pl.when(has_prev)
+    def _():
+        for back in range(1, reach):
+            @pl.when(place >= back)
+            def _():
+                agg_copy(back).wait_recv()
+
+        for dest in range(2):
+            for which in range(2):
+                total = part_out[reach, dest, which].astype(jnp.float32)
+                for back in range(1, reach):
+                    total = total + agg_in[back, dest, which].astype(jnp.float32)
+                agg_out[dest, which] = total.astype(agg_out.dtype)
+            agg_out_copy(dest, m).start()
+
     outputs(m)
     stores = [
         pltpu.make_async_copy(att_buf.at[m], att_hbm.at[:, own_cols], out_sem.at[0]),
@@ -258,11 +384,17 @@
 
     part_in[0, m] = part_out[0, m]
     part_copy(0, m, other).wait_recv()
-    for j in range(1, reach + 1):
-        @pl.when(later(j))
+    for j in range(1, reach):
+        @pl.when(sends_to(j))
         def _():
             for sender in range(2):
                 part_copy(j, m, sender).wait_recv()
+
+    @pl.when(has_next)
+    def _():
+        for sender in range(2):
+            agg_out_copy(m, sender).wait_recv()
+
     for which, ref in enumerate((dk_ref, dv_ref)):
         for e in range(2):
             total = part_in[0, e, which].astype(jnp.float32)
@@ -282,16 +414,32 @@
         copy.wait_send()
     part_copy(0, other, m).wait_send()
     for j in range(1, reach + 1):
-        @pl.when(later(j))
+        @pl.when(sends_to(j))
         def _():
             for dest in range(2):
                 for copy in kv_copy(j, dest, m):
                     copy.wait_send()
 
-        @pl.when(earlier(j))
+    for j in range(1, reach):
+        @pl.when(place >= j)
         def _():
             for dest in range(2):
                 part_copy(j, dest, m).wait_send()
+
+        @pl.when((place < j) & has_prev)
+        def _():
+            agg_copy(reach - j).wait_send()
+
+        @pl.when((place >= j) & has_prev)
+        def _():
+            for sender in range(2):
+                for which in range(2):
+                    relay_copy(j, sender, which).wait_send()
+
+    @pl.when(has_prev)
+    def _():
+        for dest in range(2):
+            agg_out_copy(dest, m).wait_send()
 
 
 def solution(mesh):
@@ -329,10 +477,19 @@
                 pltpu.VMEM((D, window), bf16),
                 pltpu.VMEM((D, window), bf16),
                 pltpu.VMEM((2, span, T), f32),
+                pltpu.VMEM((2, span, heads * T), f32),
+                pltpu.VMEM((2, span, heads * T), f32),
                 pltpu.VMEM((2, span, heads * T), bf16),
                 pltpu.VMEM((2, span, heads * T), bf16),
+                pltpu.VMEM((reach + 1, 2, 1, heads * T), f32),
+                pltpu.VMEM((reach + 1, 2, 1, heads * T), f32),
+                pltpu.VMEM((reach + 1, 2, 1, heads * T), f32),
+                pltpu.VMEM((reach + 1, 2, 1, heads * T), f32),
+                pltpu.VMEM((2, 1, heads * T), f32),
                 pltpu.VMEM((reach + 1, 2, 2, T, D), bf16),
                 pltpu.VMEM((reach + 1, 2, 2, T, D), bf16),
+                pltpu.VMEM((reach, 2, 2, T, D), bf16),
+                pltpu.VMEM((2, 2, T, D), bf16),
                 pltpu.VMEM((2, T, heads * D), bf16),
                 pltpu.VMEM((2, T, heads * D), bf16),
                 dma((4,)),
@@ -340,14 +497,17 @@
                 dma(((reach + 1) * 4,)),
                 dma((2,)),
                 dma((2,)),
+                dma((reach * 4,)),
                 dma(((reach + 1) * 2,)),
                 dma(((reach + 1) * 2,)),
+                dma((reach,)),
+                dma((reach,)),
                 dma((2,)),
                 dma((2,)),
                 dma((2,)),
             ],
             compiler_params=pltpu.CompilerParams(
-                collective_id=0, has_side_effects=True, vmem_limit_bytes=48 * 1024 * 1024
+                collective_id=0, has_side_effects=True, vmem_limit_bytes=60 * 1024 * 1024
             ),
         )(queries, out_grad, key_states, value_states, doc_lengths)
 

time: 52 us -> 39.9 us (0.77)
  the two profiles are of different devices: /device:TPU:7 before, /device:TPU:15 now
where the time goes in v2:
time: 39.9 us; the launch traced here: 39.7 us
  Pallas kernels  34.7 us (87%)
  local copies, waits for them, and re-layouts  4.3 us (11%)
  between operations  0.65 us (2%)
    pallas_call x1, Pallas kernels, body(): pl.pallas_call(functools.partial(kernel, n_ctx, reach, heads), out_shape=...  34.7 us
    unnamed x10, local copies, waits for them, and re-layouts  4.3 us

profile of v2, /device:TPU:15, one launch (start us, length us, event | category | flops | bytes accessed | tf_op | source)
XLA Modules:
  0.0 39.7 jit_solution(1023361505280166467)
XLA Ops:
  0.6 34.7 %shard_map.84 = (bf16[128,2048]{1,0:T(8,128)(2,1)}, bf16[128,2048]{1,0:T(8,128)(2,1)}, bf16[128,256]{1,0:T(8,128)(2,1)}, bf16[128,256]{1,0:T(8,128)(2,1)}) custom-call(bf16[128,2048]{1,0:T(8,128)(2,1)} %q_hbm.1, bf16[128,2048]{1,0:T(8,128)(2,1)} %g_hbm.1, bf16[128,256]{1,0:T(8,128)(2,1)} %k_hbm.1, bf16[128,256]{1,0:T(8,128)(2,1)} %v_hbm.1, s32[8]{0:T(128)} %doc_ref.1), custom_call_target="tpu_custom_call" | custom-call | tf_op jit(solution)/shard_map/pallas_call | solution.py:460
  35.4 0.0 copy-start
  35.4 1.9 %copy.13 = bf16[128,2048]{1,0:T(8,128)(2,1)} copy(bf16[128,2048]{1,0:T(8,128)(2,1)} %get-tuple-element.8) | data formatting | bytes 1048576
  37.3 0.0 copy-done
  37.3 0.0 copy-start.2
  37.3 0.8 %copy.14 = bf16[128,2048]{1,0:T(8,128)(2,1)} copy(bf16[128,2048]{1,0:T(8,128)(2,1)S(1)} %copy-done) | data formatting | bytes 1048576
  38.1 0.1 copy-done.2
  38.2 0.0 copy-start.1
  38.2 0.6 %copy.15 = bf16[128,256]{1,0:T(8,128)(2,1)} copy(bf16[128,256]{1,0:T(8,128)(2,1)S(1)} %copy-done.2) | data formatting | bytes 131072
  38.8 0.2 copy-done.1
  39.0 0.6 %copy.16 = bf16[128,256]{1,0:T(8,128)(2,1)} copy(bf16[128,256]{1,0:T(8,128)(2,1)S(1)} %copy-done.1) | data formatting | bytes 131072
Async XLA Ops:
  35.4 2.0 %copy-start = (bf16[128,2048]{1,0:T(8,128)(2,1)S(1)}, bf16[128,2048]{1,0:T(8,128)(2,1)}, u32[]{:S(2)}) copy-start(bf16[128,2048]{1,0:T(8,128)(2,1)} %get-tuple-element.9) | copy-start | bytes 1572868
  37.3 0.9 %copy-start.2 = (bf16[128,256]{1,0:T(8,128)(2,1)S(1)}, bf16[128,256]{1,0:T(8,128)(2,1)}, u32[]{:S(2)}) copy-start(bf16[128,256]{1,0:T(8,128)(2,1)} %get-tuple-element.10) | copy-start | bytes 196612
  38.2 0.9 %copy-start.1 = (bf16[128,256]{1,0:T(8,128)(2,1)S(1)}, bf16[128,256]{1,0:T(8,128)(2,1)}, u32[]{:S(2)}) copy-start(bf16[128,256]{1,0:T(8,128)(2,1)} %get-tuple-element.11) | copy-start | bytes 196612

commit v3 on v2

--- a/solution.py
+++ b/solution.py
@@ -10,7 +10,8 @@
 
 HEAD_DIM = 128
 DOC_MAX = 1024
-STEP = 512
+STEP = 1024
+VMEM_LIMIT = 60 * 1024 * 1024
 MESH = pl.DeviceIdType.MESH
 
 
@@ -48,8 +49,20 @@
     has_next = c + reach < n_ctx
     has_prev = c >= reach
 
+    def crosses_to(j):
+        return has_next & (2 * place + j == 2 * reach - 1)
+
+    def crosses_from(j):
+        return has_prev & (2 * place + 1 == j)
+
     def sends_to(j):
-        return has_next if j == reach else place + j < reach
+        return has_next if j == reach else (place + j < reach) | crosses_to(j)
+
+    def direct_back(j):
+        return (place >= j) | crosses_from(j)
+
+    def relays(back):
+        return has_prev & (place >= back) & (2 * place - back != reach - 1)
 
     def exists(j):
         return c >= j
@@ -60,6 +73,16 @@
         for e in range(2):
             near = c - place + (place + j) % reach
             pl.semaphore_signal(barrier, inc=1, device_id=(near, e), device_id_type=MESH)
+
+        @pl.when(crosses_to(j))
+        def _():
+            for e in range(2):
+                pl.semaphore_signal(barrier, inc=1, device_id=(c + j, e), device_id_type=MESH)
+
+        @pl.when(crosses_from(j))
+        def _():
+            for e in range(2):
+                pl.semaphore_signal(barrier, inc=1, device_id=(c - j, e), device_id_type=MESH)
 
     @pl.when(has_next)
     def _():
@@ -84,6 +107,8 @@
         copy.start()
 
     peers = 1 + 2 * (reach - 1) + jnp.where(has_next, 2, 0) + jnp.where(has_prev, 2, 0)
+    for j in range(1, reach):
+        peers = peers + jnp.where(crosses_to(j), 2, 0) + jnp.where(crosses_from(j), 2, 0)
     pl.semaphore_wait(barrier, peers)
 
     def kv_copy(j, dest, sender):
@@ -160,7 +185,7 @@
             part_in[j] = jnp.zeros(part_in.shape[1:], part_in.dtype)
 
     for back in range(1, reach):
-        @pl.when(place < back)
+        @pl.when(jnp.logical_not(relays(back)))
         def _():
             agg_in[back] = jnp.zeros(agg_in.shape[1:], agg_in.dtype)
 
@@ -174,6 +199,16 @@
         key_pos = (c - reach) * shard + t * T + lax.broadcasted_iota(jnp.int32, (span, T), 0)
         allowed = (key_pos >= first) & (key_pos <= row_pos)
         bias[t] = jnp.where(allowed, 0.0, -1e30)
+
+    @pl.when(has_prev)
+    def _():
+        for sender in range(2):
+            for which, copy in enumerate(kv_copy(reach, m, sender)):
+                copy.wait_recv()
+                for back in range(1, reach):
+                    @pl.when(relays(back))
+                    def _():
+                        relay_copy(back, sender, which).start()
 
     for copy in loads:
         copy.wait()
@@ -222,16 +257,6 @@
         copy.wait_recv()
     score_block(0)
 
-    @pl.when(has_prev)
-    def _():
-        for sender in range(2):
-            for which, copy in enumerate(kv_copy(reach, m, sender)):
-                copy.wait_recv()
-                for back in range(1, reach):
-                    @pl.when(place >= back)
-                    def _():
-                        relay_copy(back, sender, which).start()
-
     score_block(reach)
     for j in range(1, reach):
         @pl.when(exists(j))
@@ -284,7 +309,7 @@
             device_id_type=MESH,
         )
 
-    for j in range(reach, -1, -1):
+    for j in (*range(reach - 1, 0, -1), reach, 0):
         for t in range(2):
             low, high = rows_of(j, t)
 
@@ -313,18 +338,19 @@
         if j == 0:
             part_copy(0, other, m).start()
         elif j < reach:
-            @pl.when(place >= j)
+            @pl.when(direct_back(j))
             def _():
                 for dest in range(2):
                     part_copy(j, dest, m).start()
 
-            @pl.when((place < j) & has_prev)
+            @pl.when((place < j) & has_prev & (2 * place + 1 != j))
             def _():
                 agg_copy(reach - j).start()
 
     kwin_t[...] = kwin[...].T
     vwin_t[...] = vwin[...].T
-    pair = 2 * T
+    out_heads = min(4, heads)
+    pair = out_heads * T
 
     def remote_out(sender, dest):
         cols = pl.ds(pl.multiple_of(sender * half_cols, D), half_cols)
@@ -347,13 +373,13 @@
             cols = pl.ds(pl.multiple_of(i * pair, pair), pair)
             o = dot_plain(vwin_t[:, keys], probs[t, :, cols]).T
             dq = (dot_plain(kwin_t[:, keys], dscores[t, :, cols]) * factor).T
-            for a in range(2):
-                at = pl.ds(pl.multiple_of(i * 2 * D + a * D, D), D)
+            for a in range(out_heads):
+                at = pl.ds(pl.multiple_of(i * pair + a * D, D), D)
                 att_buf[t, :, at] = o[a * T : (a + 1) * T].astype(att_buf.dtype)
                 dq_buf[t, :, at] = dq[a * T : (a + 1) * T].astype(dq_buf.dtype)
             return carry
 
-        lax.fori_loop(0, heads // 2, one_pair, 0)
+        lax.fori_loop(0, heads // out_heads, one_pair, 0)
 
     outputs(other)
     for copy in remote_out(m, other):
@@ -362,7 +388,7 @@
     @pl.when(has_prev)
     def _():
         for back in range(1, reach):
-            @pl.when(place >= back)
+            @pl.when(relays(back))
             def _():
                 agg_copy(back).wait_recv()
 
@@ -421,16 +447,16 @@
                     copy.wait_send()
 
     for j in range(1, reach):
-        @pl.when(place >= j)
+        @pl.when(direct_back(j))
         def _():
             for dest in range(2):
                 part_copy(j, dest, m).wait_send()
 
-        @pl.when((place < j) & has_prev)
+        @pl.when((place < j) & has_prev & (2 * place + 1 != j))
         def _():
             agg_copy(reach - j).wait_send()
 
-        @pl.when((place >= j) & has_prev)
+        @pl.when(relays(j))
         def _():
             for sender in range(2):
                 for which in range(2):
@@ -440,6 +466,20 @@
     def _():
         for dest in range(2):
             agg_out_copy(dest, m).wait_send()
+
+
+def place_results(*refs):
+    sources, results, held = refs[:4], refs[4:8], refs[8:12]
+    in_sem, out_sem = refs[12:]
+    fetches = [pltpu.make_async_copy(sources[i], held[i], in_sem.at[i]) for i in range(4)]
+    stores = [pltpu.make_async_copy(held[i], results[i], out_sem.at[i]) for i in range(4)]
+    for copy in fetches:
+        copy.start()
+    for i in range(4):
+        fetches[i].wait()
+        stores[i].start()
+    for copy in stores:
+        copy.wait()
 
 
 def solution(mesh):
@@ -457,7 +497,7 @@
         hbm = pl.BlockSpec(memory_space=pl.ANY)
         vmem = pl.BlockSpec(memory_space=pltpu.VMEM)
         dma = pltpu.SemaphoreType.DMA
-        return pl.pallas_call(
+        results = pl.pallas_call(
             functools.partial(kernel, n_ctx, reach, heads),
             out_shape=(
                 jax.ShapeDtypeStruct(queries.shape, bf16),
@@ -507,9 +547,17 @@
                 dma((2,)),
             ],
             compiler_params=pltpu.CompilerParams(
-                collective_id=0, has_side_effects=True, vmem_limit_bytes=60 * 1024 * 1024
+                collective_id=0, has_side_effects=True, vmem_limit_bytes=VMEM_LIMIT
             ),
         )(queries, out_grad, key_states, value_states, doc_lengths)
+        return pl.pallas_call(
+            place_results,
+            out_shape=tuple(jax.ShapeDtypeStruct(x.shape, x.dtype) for x in results),
+            in_specs=[hbm] * 4,
+            out_specs=(hbm,) * 4,
+            scratch_shapes=[pltpu.VMEM(x.shape, x.dtype) for x in results] + [dma((4,)), dma((4,))],
+            compiler_params=pltpu.CompilerParams(vmem_limit_bytes=VMEM_LIMIT),
+        )(*results)
 
     return jax.shard_map(
         body,

time: 39.9 us -> 34.5 us (0.86)
  the two profiles are of different devices: /device:TPU:15 before, /device:TPU:13 now
where the time goes in v3:
time: 34.5 us; the launch traced here: 34.4 us
  Pallas kernels  33.7 us (98%)
  between operations  0.64 us (2%)
    pallas_call x1, Pallas kernels, body(): pl.pallas_call(functools.partial(kernel, n_ctx, reach, heads), out_shape=...  31.6 us
    pallas_call x1, Pallas kernels, body(): pl.pallas_call(place_results, out_shape=tuple((jax.ShapeDtypeStruct(x.sha...  2.11 us

profile of v3, /device:TPU:13, one launch (start us, length us, event | category | flops | bytes accessed | tf_op | source)
XLA Modules:
  0.0 34.4 jit_solution(9530787591676549674)
XLA Ops:
  0.6 31.6 %shard_map.84 = (bf16[128,2048]{1,0:T(8,128)(2,1)}, bf16[128,2048]{1,0:T(8,128)(2,1)}, bf16[128,256]{1,0:T(8,128)(2,1)}, bf16[128,256]{1,0:T(8,128)(2,1)}) custom-call(bf16[128,2048]{1,0:T(8,128)(2,1)} %q_hbm.1, bf16[128,2048]{1,0:T(8,128)(2,1)} %g_hbm.1, bf16[128,256]{1,0:T(8,128)(2,1)} %k_hbm.1, bf16[128,256]{1,0:T(8,128)(2,1)} %v_hbm.1, s32[8]{0:T(128)} %doc_ref.1), custom_call_target="tpu_custom_call" | custom-call | tf_op jit(solution)/shard_map/pallas_call | solution.py:500
  32.3 2.1 %shard_map.85 = (bf16[128,2048]{1,0:T(8,128)(2,1)}, bf16[128,2048]{1,0:T(8,128)(2,1)}, bf16[128,256]{1,0:T(8,128)(2,1)}, bf16[128,256]{1,0:T(8,128)(2,1)}) custom-call(bf16[128,2048]{1,0:T(8,128)(2,1)} %get-tuple-element.8.refs_0_, bf16[128,2048]{1,0:T(8,128)(2,1)} %get-tuple-element.9.refs_1_, bf16[128,256]{1,0:T(8,128)(2,1)} %get-tuple-element.10.refs_2_, ...), custom_call_target="tpu_custom_call" | custom-call | tf_op jit(solution)/shard_map/pallas_call | solution.py:553

commit v4 on v3

--- a/solution.py
+++ b/solution.py
@@ -289,12 +289,12 @@
             device_id_type=MESH,
         )
 
-    def agg_copy(back):
+    def agg_copy(back, half):
         return pltpu.make_async_remote_copy(
-            src_ref=part_out.at[reach - back],
-            dst_ref=agg_in.at[back],
-            send_sem=agg_send.at[back],
-            recv_sem=agg_recv.at[back],
+            src_ref=part_out.at[reach - back, half],
+            dst_ref=agg_in.at[back, half],
+            send_sem=agg_send.at[back * 2 + half],
+            recv_sem=agg_recv.at[back * 2 + half],
             device_id=(c + back, m),
             device_id_type=MESH,
         )
@@ -345,7 +345,8 @@
 
             @pl.when((place < j) & has_prev & (2 * place + 1 != j))
             def _():
-                agg_copy(reach - j).start()
+                for half in range(2):
+                    agg_copy(reach - j, half).start()
 
     kwin_t[...] = kwin[...].T
     vwin_t[...] = vwin[...].T
@@ -387,12 +388,12 @@
 
     @pl.when(has_prev)
     def _():
-        for back in range(1, reach):
-            @pl.when(relays(back))
-            def _():
-                agg_copy(back).wait_recv()
-
         for dest in range(2):
+            for back in range(1, reach):
+                @pl.when(relays(back))
+                def _():
+                    agg_copy(back, dest).wait_recv()
+
             for which in range(2):
                 total = part_out[reach, dest, which].astype(jnp.float32)
                 for back in range(1, reach):
@@ -454,7 +455,8 @@
 
         @pl.when((place < j) & has_prev & (2 * place + 1 != j))
         def _():
-            agg_copy(reach - j).wait_send()
+            for half in range(2):
+                agg_copy(reach - j, half).wait_send()
 
         @pl.when(relays(j))
         def _():
@@ -540,8 +542,8 @@
                 dma((reach * 4,)),
                 dma(((reach + 1) * 2,)),
                 dma(((reach + 1) * 2,)),
-                dma((reach,)),
-                dma((reach,)),
+                dma((reach * 2,)),
+                dma((reach * 2,)),
                 dma((2,)),
                 dma((2,)),
                 dma((2,)),

time: 34.5 us -> 33.9 us (0.983)
  Pallas kernels: 33.7 us -> 33.1 us
    pallas_call x1, Pallas kernels: 31.6 us -> 31 us  [body(): pl.pallas_call(functools.partial(kernel, n_ctx, reach, heads), out_shape=...]
where the time goes in v4:
time: 33.9 us; the launch traced here: 33.7 us
  Pallas kernels  33.1 us (98%)
  between operations  0.64 us (2%)
    pallas_call x1, Pallas kernels, body(): pl.pallas_call(functools.partial(kernel, n_ctx, reach, heads), out_shape=...  31 us
    pallas_call x1, Pallas kernels, body(): pl.pallas_call(place_results, out_shape=tuple((jax.ShapeDtypeStruct(x.sha...  2.11 us

profile of v4, /device:TPU:13, one launch (start us, length us, event | category | flops | bytes accessed | tf_op | source)
XLA Modules:
  0.0 33.7 jit_solution(2850685145739027496)
XLA Ops:
  0.6 31.0 %shard_map.84 = (bf16[128,2048]{1,0:T(8,128)(2,1)}, bf16[128,2048]{1,0:T(8,128)(2,1)}, bf16[128,256]{1,0:T(8,128)(2,1)}, bf16[128,256]{1,0:T(8,128)(2,1)}) custom-call(bf16[128,2048]{1,0:T(8,128)(2,1)} %q_hbm.1, bf16[128,2048]{1,0:T(8,128)(2,1)} %g_hbm.1, bf16[128,256]{1,0:T(8,128)(2,1)} %k_hbm.1, bf16[128,256]{1,0:T(8,128)(2,1)} %v_hbm.1, s32[8]{0:T(128)} %doc_ref.1), custom_call_target="tpu_custom_call" | custom-call | tf_op jit(solution)/shard_map/pallas_call | solution.py:502
  31.6 2.1 %shard_map.85 = (bf16[128,2048]{1,0:T(8,128)(2,1)}, bf16[128,2048]{1,0:T(8,128)(2,1)}, bf16[128,256]{1,0:T(8,128)(2,1)}, bf16[128,256]{1,0:T(8,128)(2,1)}) custom-call(bf16[128,2048]{1,0:T(8,128)(2,1)} %get-tuple-element.8.refs_0_, bf16[128,2048]{1,0:T(8,128)(2,1)} %get-tuple-element.9.refs_1_, bf16[128,256]{1,0:T(8,128)(2,1)} %get-tuple-element.10.refs_2_, ...), custom_call_target="tpu_custom_call" | custom-call | tf_op jit(solution)/shard_map/pallas_call | solution.py:555
